TPU v7x, 32 devices: a whole 2x2x4 slice. The times are simulated.
32 devices in a mesh: ga: 8 (over y, x, core), ba: 4 (over z).
Axes of the slice: x: 2, y: 2, z: 4, core: 2. Of those that a mesh axis runs over, the one named last changes fastest.
Arguments:
- pairs: bfloat16 [48, 64, 4096], P('ba', None, 'ga'), may hold values from -0.059814453 to 0.059814453
- dielectric: bfloat16 [4, 4096, 4096], P(None, 'ga'), may hold values from -0.5 to 1.5, as said below
- freq_weight: float32 [4, 48], P(None, 'ba'), may hold values from 0.1 to 1
- shells: int32 [4096], P('ga'), may hold values from 0 to 63
Outputs:
- sigma: float32 [4, 64, 64], P(None, 'ba')
Inputs may be any that keep to these rules, and one draw needn't show every extreme that they name: `dielectric`: each frequency's matrix is its diagonal plus small full-rank off-diagonal entries; the diagonal lies between 0.5 and 1.5.
All inputs are finite; a program needn't handle non-finite values.
Results may differ from a plain program's by a relative error of at most 0.0003.
Values may be sent and summed in bfloat16 or wider, within the bound.
A program may use at most 64 MiB of HBM per device.

v0:
```python
import jax
import jax.numpy as jnp
from jax import lax
from jax.sharding import PartitionSpec as P


def local(pairs, dielectric, freq_weight, shells):
    coulomb = lax.rsqrt(shells.astype(jnp.float32) + 1.0)
    scaled = (pairs.astype(jnp.float32) * coulomb).astype(jnp.bfloat16)
    num_freq, local_rows, all_columns = dielectric.shape
    summed_bands, bands, own_width = scaled.shape
    row_matrix = dielectric.reshape(num_freq * local_rows, all_columns)
    piece = lax.all_gather(scaled, "ga", axis=2, tiled=True)
    count = piece.shape[2]
    flat_piece = piece.reshape(summed_bands * bands, count)
    applied = lax.dot_general(
        row_matrix, flat_piece, (((1,), (1,)), ((), ())), preferred_element_type=jnp.float32
    )
    applied = applied.reshape(num_freq, local_rows, summed_bands, bands)
    applied = applied * freq_weight[:, None, :, None]
    partial_value = jnp.einsum(
        "kng,fgkm->fnm", scaled.astype(jnp.float32), applied, precision=lax.Precision.HIGHEST
    )
    summed = lax.psum(partial_value, "ga")
    result = lax.psum_scatter(summed, "ba", scatter_dimension=1, tiled=True)
    return result


def solution(mesh):
    in_specs = (P("ba", None, "ga"), P(None, "ga", None), P(None, "ba"), P("ga"))
    out_specs = P(None, "ba", None)
    return jax.shard_map(local, mesh=mesh, in_specs=in_specs, out_specs=out_specs, check_vma=False)
```

profile of v0, /device:TPU:0, one launch (start us, length us, event | category | flops | bytes accessed | tf_op | source)
XLA Modules:
  0.0 161.1 jit_solution(11373394748133110843)
XLA Ops:
  6.5 0.0 all-gather.2.cloned.1.call-start
  6.5 0.7 add_rsqrt_fusion
  7.2 2.2 %multiply_convert_fusion = bf16[12,64,512]{2,1,0:T(8,128)(2,1)} fusion(bf16[12,64,512]{2,1,0:T(8,128)(2,1)} %param.4, f32[512]{0:T(512)S(1)} %add_rsqrt_fusion), kind=kLoop, calls=%fused_computation.4 | loop fusion | flops 1179648 | bytes 1574912 | tf_op jit(solution)/shard_map/convert_element_type | solution.py:9
  9.4 0.0 all-gather.2.cloned.1.call-update
  9.5 0.0 all-reduce.3.cloned.1.call-start
  9.5 49.5 %all-gather.2.cloned.1.call-done = bf16[12,64,4096]{2,1,0:T(8,128)(2,1)} async-done(((bf16[12,64,512]{2,1,0:T(8,128)(2,1)}), bf16[12,64,4096]{2,1,0:T(8,128)(2,1)}) %all-gather.2.cloned.1.call-update) | async-done | bytes 6291472 | tf_op jit(solution)/shard_map/all_gather | solution.py:13
  59.0 20.2 %convolution_bitcast_fusion = f32[2048,768]{0,1:T(8,128)} fusion(bf16[768,4096]{1,0:T(8,128)(2,1)} %bitcast.18, bf16[2048,4096]{1,0:T(8,128)(2,1)} %bitcast.17), kind=kOutput, calls=%fused_computation.2 | convolution fusion | flops 12884901888 | bytes 29360128 | tf_op jit(solution)/shard_map/dot_general | solution.py:16
  79.2 0.0 copy-start
  79.2 0.0 copy-start.1
  79.2 8.5 %reshape.13 = f32[4,512,12,64]{1,0,3,2:T(4,128)} reshape(f32[2048,768]{0,1:T(8,128)} %convolution_bitcast_fusion) | data formatting | bytes 12582912 | tf_op jit(solution)/shard_map/reshape | solution.py:19
  87.7 0.0 copy-done
  87.7 0.0 copy-done.1
  87.7 0.0 copy-start.2
  87.7 7.4 %fusion.2 = f32[4,64,64]{1,2,0:T(8,128)S(1)} fusion(f32[4,512,12,64]{1,0,3,2:T(4,128)} %reshape.13, f32[4,12]{1,0:T(4,128)S(1)} %copy-done.1, bf16[12,64,512]{2,1,0:T(8,128)(2,1)S(1)} %copy-done), kind=kOutput, calls=%fused_computation.5 | convolution fusion | flops 1209532416 | bytes 7143616 | tf_op jit(solution)/shard_map/kng,fgkm->fnm/dot_general | solution.py:21
  95.1 0.7 copy.8
  95.9 0.0 all-reduce.3.cloned.1.call-update
  95.9 0.0 copy-done.2
  95.9 0.6 dynamic-slice
  97.1 33.4 %all-reduce.3.cloned.1.call-done = f32[4,64,64]{2,0,1:T(4,128)} async-done(((f32[4,64,64]{2,0,1:T(4,128)}), f32[4,64,64]{2,0,1:T(4,128)}) %all-reduce.3.cloned.1.call-update) | async-done | bytes 65552
  130.5 0.8 constant_dynamic-slice_fusion
  131.3 22.3 %psum.8 = f32[4,16,64]{2,0,1:T(4,128)S(1)} all-reduce(f32[4,16,64]{2,0,1:T(4,128)S(1)} %constant_dynamic-slice_fusion), channel_id=1, replica_groups=mesh['ga'=8,'ba'=4] {'ga'}, use_global_device_ids=true, to_apply=%region_0.0 | all-reduce | flops 4096 | bytes 32768 | tf_op jit(solution)/shard_map/psum | solution.py:24
  153.6 0.6 copy.9
Async XLA Ops:
  6.5 52.5 %all-gather.2.cloned.1.call-start = ((), (), s32[]{:S(2)}) async-start(), calls=%async_computation | async-start | bytes 7077888 | tf_op jit(solution)/shard_map/all_gather | solution.py:13
  9.5 121.0 %all-reduce.3.cloned.1.call-start = ((), (), s32[]{:S(2)}) async-start(), calls=%async_computation.1 | async-start | bytes 262144
  79.2 8.5 %copy-start = (bf16[12,64,512]{2,1,0:T(8,128)(2,1)S(1)}, bf16[12,64,512]{2,1,0:T(8,128)(2,1)}, u32[]{:S(2)}) copy-start(bf16[12,64,512]{2,1,0:T(8,128)(2,1)} %multiply_convert_fusion) | copy-start | bytes 2359300
  79.2 8.5 %copy-start.1 = (f32[4,12]{1,0:T(4,128)S(1)}, f32[4,12]{1,0:T(4,128)}, u32[]{:S(2)}) copy-start(f32[4,12]{1,0:T(4,128)} %param.6) | copy-start | bytes 580
  87.7 8.2 %copy-start.2 = (u32[32]{0:T(128)S(1)}, u32[32]{0:T(128)}, u32[]{:S(2)}) copy-start(u32[32]{0:T(128)} %constant.4) | copy-start | bytes 388
Sparse Core Ops, SparseCore 0:
  9.6 49.3 all-gather.1
  96.0 34.4 all-reduce.2
where the time goes:
time: 161 us
  waiting for transfers between devices  82.9 us (51%)
  matrix products  27.6 us (17%)
  blocking collectives  22.3 us (14%)
  between operations  14.1 us (9%)
  local copies, waits for them, and re-layouts  11.2 us (7%)
  other arithmetic  2.91 us (2%)
    all_gather x1, waiting for transfers between devices, local(): piece = lax.all_gather(scaled, 'ga', axis=2, tiled=True)  49.5 us
    unnamed x3, waiting for transfers between devices  33.4 us
    psum x1, blocking collectives, local(): summed = lax.psum(partial_value, 'ga')  22.3 us
    dot_general x1, matrix products, local(): lax.dot_general(row_matrix, flat_piece, (((1,), (1,)), ((), ())), preferr...  20.2 us
    reshape x1, local copies, waits for them, and re-layouts, local(): applied = applied.reshape(num_freq, local_rows, summed_bands, bands)  8.48 us
    dot_general x1, matrix products, local(): jnp.einsum('kng,fgkm->fnm', scaled.astype(jnp.float32), applied, precisio...  7.44 us
  transfers between devices with their start and end apart: 2, of which 2 were waited for; matrix products, arithmetic and copies ran while one was open for 0% of the time, Pallas kernels for 0%

commit v1 on v0

--- a/solution.py
+++ b/solution.py
@@ -1,7 +1,16 @@
+import functools
+
 import jax
 import jax.numpy as jnp
 from jax import lax
+from jax.experimental import pallas as pl
+from jax.experimental.pallas import tpu as pltpu
 from jax.sharding import PartitionSpec as P
+
+MESH = pl.DeviceIdType.MESH
+CHUNKS = 4
+NT = (((1,), (1,)), ((), ()))
+NN = (((1,), (0,)), ((), ()))
 
 
 def local(pairs, dielectric, freq_weight, shells):
@@ -26,7 +35,333 @@
     return result
 
 
+def kernel(
+    pairs_hbm, d_hbm, w_ref, shells_ref, out_ref,
+    raw, s, d, acc_a, hl, acc, acc_t, red_src, red_recv, red_all,
+    pairs_sem, d_sem, send_sem, recv_sem, relay_send, red_send, red_rsem, all_send, all_rsem,
+):
+    num_k, bands, width = raw.shape
+    num_freq = d.shape[1]
+    num_ba = red_src.shape[0]
+    per = num_k // CHUNKS
+    a = lax.axis_index("ga")
+    b = lax.axis_index("ba")
+    y, x, c = a // 4, (a // 2) % 2, a % 2
+
+    def partner(mask):
+        py = 1 - y if mask & 4 else y
+        px = 1 - x if mask & 2 else x
+        pc = 1 - c if mask & 1 else c
+        return py * 4 + px * 2 + pc
+
+    relay_to = (y + (1 - c) * (1 - 2 * y)) * 4 + (x + c * (1 - 2 * x)) * 2 + c
+    relay_slot = 2 + 2 * c
+
+    pairs_copies = []
+    for j in range(CHUNKS):
+        copy = pltpu.make_async_copy(
+            pairs_hbm.at[pl.ds(j * per, per)], raw.at[pl.ds(j * per, per)], pairs_sem.at[j]
+        )
+        copy.start()
+        pairs_copies.append(copy)
+    d_copies = {}
+    for slot in (0, 1, 6, 7, 2, 4, 3, 5):
+        columns = pl.ds(pl.multiple_of(partner(slot) * width, width), width)
+        d_copies[slot] = pltpu.make_async_copy(d_hbm.at[:, :, columns], d.at[slot], d_sem.at[slot])
+        d_copies[slot].start()
+
+    barrier = pltpu.get_barrier_semaphore()
+    for mask in range(1, 8):
+        pl.semaphore_signal(barrier, inc=1, device_id={"ga": partner(mask)}, device_id_type=MESH)
+    for step in range(1, num_ba):
+        pl.semaphore_signal(
+            barrier, inc=1, device_id={"ba": (b + step) % num_ba}, device_id_type=MESH
+        )
+
+    coulomb = lax.rsqrt(shells_ref[...].astype(jnp.float32) + 1.0)
+
+    def scale(j):
+        pairs_copies[j].wait()
+        rows = pl.ds(j * per, per)
+        wide = raw[rows].reshape(per * bands, width).astype(jnp.float32) * coulomb
+        s[0, rows] = wide.astype(jnp.bfloat16).reshape(per, bands, width)
+
+    def send(src_slot, mask, dst_slot, j, sem):
+        rows = pl.ds(j * per, per)
+        target = relay_to if mask is None else partner(mask)
+        copy = pltpu.make_async_remote_copy(
+            src_ref=s.at[src_slot, rows],
+            dst_ref=s.at[dst_slot, rows],
+            send_sem=sem,
+            recv_sem=recv_sem.at[dst_slot, j],
+            device_id={"ga": target},
+            device_id_type=MESH,
+        )
+        copy.start()
+        return copy
+
+    started = []
+
+    def forward(slot, mask, dst_slot, j):
+        started.append(send(slot, mask, dst_slot, j, send_sem.at[dst_slot, j]))
+
+    arrived = set()
+
+    def wait(slot, j):
+        if slot == 0 or (slot, j) in arrived:
+            return
+        arrived.add((slot, j))
+        rows = pl.ds(j * per, per)
+        pltpu.make_async_remote_copy(
+            src_ref=s.at[slot, rows], dst_ref=s.at[slot, rows],
+            send_sem=send_sem.at[slot, j], recv_sem=recv_sem.at[slot, j],
+            device_id={"ga": partner(1)}, device_id_type=MESH,
+        ).wait_recv()
+
+    ready = set()
+
+    def need(slot):
+        if slot not in ready:
+            ready.add(slot)
+            d_copies[slot].wait()
+
+    def arrive(j):
+        wait(2, j)
+        forward(2, 1, 3, j)
+        wait(4, j)
+        forward(relay_slot, None, 6, j)
+        forward(4, 1, 5, j)
+
+    def arrive_far(j):
+        wait(6, j)
+        forward(6, 1, 7, j)
+
+    def apply_h(slots, first, parts):
+        for slot in slots:
+            need(slot)
+        size = per * parts[1]
+        start = parts[0] * per
+
+        def body(f, carry):
+            total = None
+            for slot in slots:
+                left = s[slot, pl.ds(start, size)].reshape(size * bands, width)
+                term = lax.dot_general(left, d[slot, f], NT, preferred_element_type=jnp.float32)
+                total = term if total is None else total + term
+            total = total.reshape(size, bands, width)
+            if first:
+                acc_a[pl.ds(start, size), f] = total
+            else:
+                acc_a[pl.ds(start, size), f] += total
+            return carry
+
+        lax.fori_loop(0, num_freq, body, 0)
+
+    def split(which, rows, f, wide):
+        high = wide.astype(jnp.bfloat16)
+        low = (wide - high.astype(jnp.float32)).astype(jnp.bfloat16)
+        hl[which, rows, 0, f] = high
+        hl[which, rows, 1, f] = low
+
+    def apply_g(which, slot, half):
+        need(slot)
+        size = num_k // 2
+        rows = pl.ds(half * size, size)
+
+        def body(f, carry):
+            wide = lax.dot_general(
+                s[0, rows].reshape(size * bands, width), d[slot, f], NN,
+                preferred_element_type=jnp.float32,
+            )
+            split(which, rows, f, wide.reshape(size, bands, width))
+            return carry
+
+        lax.fori_loop(0, num_freq, body, 0)
+
+    def second(which, slot, target, j):
+        def body(k, carry):
+            left = hl[which, k].reshape(2 * num_freq * bands, width)
+            both = lax.dot_general(left, s[slot, k], NT, preferred_element_type=jnp.float32)
+            both = both.reshape(2, num_freq, bands, bands)
+            both = both[0] + both[1]
+            return tuple(carry[f] + w_ref[f, k] * both[f] for f in range(num_freq))
+
+        terms = tuple(target[f] for f in range(num_freq))
+        for k in range(j * per, (j + 1) * per):
+            terms = body(k, terms)
+        for f in range(num_freq):
+            target[f] = terms[f]
+
+    acc[...] = jnp.zeros_like(acc)
+    acc_t[...] = jnp.zeros_like(acc_t)
+
+    scale(0)
+    pl.semaphore_wait(barrier, 7 + num_ba - 1)
+    for j in range(CHUNKS):
+        if j:
+            scale(j)
+        forward(0, 2, 2, j)
+        forward(0, 4, 4, j)
+        started.append(send(0, 1, 1, j, relay_send.at[j]))
+
+    for j in range(CHUNKS):
+        wait(1, j)
+    apply_h((0, 1), True, (0, CHUNKS))
+    arrive(0)
+    apply_h((2, 4), False, (0, 1))
+    apply_g(0, 6, 0)
+    apply_g(0, 6, 1)
+    arrive(1)
+    wait(3, 0)
+    wait(5, 0)
+    apply_h((2, 4), False, (1, 1))
+    apply_h((3, 5), False, (0, 1))
+    apply_g(1, 7, 0)
+    arrive(2)
+    apply_g(1, 7, 1)
+    wait(3, 1)
+    wait(5, 1)
+    apply_h((3, 5), False, (1, 1))
+    arrive_far(0)
+    apply_h((2, 4), False, (2, 1))
+    arrive(3)
+    wait(3, 2)
+    wait(5, 2)
+    apply_h((3, 5), False, (2, 1))
+    arrive_far(1)
+    apply_h((2, 4), False, (3, 1))
+    wait(3, 3)
+    wait(5, 3)
+    apply_h((3, 5), False, (3, 1))
+    for j in range(CHUNKS):
+        rows = pl.ds(j * per, per)
+        for f in range(num_freq):
+            split(2, rows, f, acc_a[rows, f])
+        second(2, 0, acc_t, j)
+        if j == 1:
+            second(0, 6, acc, 0)
+            second(0, 6, acc, 1)
+            arrive_far(2)
+    wait(7, 0)
+    second(1, 7, acc, 0)
+    wait(7, 1)
+    second(1, 7, acc, 1)
+    second(0, 6, acc, 2)
+    arrive_far(3)
+    wait(7, 2)
+    second(1, 7, acc, 2)
+    second(0, 6, acc, 3)
+    wait(7, 3)
+    second(1, 7, acc, 3)
+
+    piece = bands // num_ba
+    for pair in range(num_freq // 2):
+        first_f = acc[2 * pair] + acc_t[2 * pair].T
+        second_f = acc[2 * pair + 1] + acc_t[2 * pair + 1].T
+        both = jnp.concatenate([first_f, second_f], axis=1)
+        red_src[:, pair] = both.reshape(num_ba, piece, 2 * bands)
+
+    red_copies = []
+    for step in range(1, num_ba):
+        to = (b + step) % num_ba
+        copy = pltpu.make_async_remote_copy(
+            src_ref=red_src.at[to], dst_ref=red_recv.at[step - 1],
+            send_sem=red_send.at[step - 1], recv_sem=red_rsem.at[step - 1],
+            device_id={"ba": to}, device_id_type=MESH,
+        )
+        copy.start()
+        red_copies.append(copy)
+    total = red_src[b]
+    for step, copy in enumerate(red_copies):
+        copy.wait_recv()
+        total = total + red_recv[step]
+    red_all[a] = total
+    all_copies = []
+    for mask in range(1, 8):
+        copy = pltpu.make_async_remote_copy(
+            src_ref=red_all.at[a], dst_ref=red_all.at[a],
+            send_sem=all_send.at[mask], recv_sem=all_rsem.at[mask],
+            device_id={"ga": partner(mask)}, device_id_type=MESH,
+        )
+        copy.start()
+        all_copies.append(copy)
+    for mask, copy in enumerate(all_copies, 1):
+        slot = partner(mask)
+        pltpu.make_async_remote_copy(
+            src_ref=red_all.at[slot], dst_ref=red_all.at[slot],
+            send_sem=all_send.at[mask], recv_sem=all_rsem.at[mask],
+            device_id={"ga": slot}, device_id_type=MESH,
+        ).wait_recv()
+    total = red_all[0]
+    for other in range(1, 8):
+        total = total + red_all[other]
+    for pair in range(num_freq // 2):
+        out_ref[2 * pair] = total[pair][:, :bands]
+        out_ref[2 * pair + 1] = total[pair][:, bands:]
+    for copy in started + red_copies + all_copies:
+        copy.wait_send()
+
+
+def fused(pairs, dielectric, freq_weight, shells, num_ba):
+    num_k, bands, width = pairs.shape
+    num_freq, rows, columns = dielectric.shape
+    bf16, f32 = jnp.bfloat16, jnp.float32
+    piece = bands // num_ba
+    dma = pltpu.SemaphoreType.DMA
+    return pl.pallas_call(
+        kernel,
+        out_shape=jax.ShapeDtypeStruct((num_freq, piece, bands), f32),
+        in_specs=[
+            pl.BlockSpec(memory_space=pl.ANY),
+            pl.BlockSpec(memory_space=pl.ANY),
+            pl.BlockSpec(memory_space=pltpu.SMEM),
+            pl.BlockSpec(memory_space=pltpu.VMEM),
+        ],
+        out_specs=pl.BlockSpec(memory_space=pltpu.VMEM),
+        scratch_shapes=[
+            pltpu.VMEM((num_k, bands, width), bf16),
+            pltpu.VMEM((8, num_k, bands, width), bf16),
+            pltpu.VMEM((8, num_freq, rows, width), bf16),
+            pltpu.VMEM((num_k, num_freq, bands, width), f32),
+            pltpu.VMEM((3, num_k, 2, num_freq, bands, width), bf16),
+            pltpu.VMEM((num_freq, bands, bands), f32),
+            pltpu.VMEM((num_freq, bands, bands), f32),
+            pltpu.VMEM((num_ba, num_freq // 2, piece, 2 * bands), f32),
+            pltpu.VMEM((num_ba - 1, num_freq // 2, piece, 2 * bands), f32),
+            pltpu.VMEM((8, num_freq // 2, piece, 2 * bands), f32),
+            dma((CHUNKS,)),
+            dma((8,)),
+            dma((8, CHUNKS)),
+            dma((8, CHUNKS)),
+            dma((CHUNKS,)),
+            dma((num_ba - 1,)),
+            dma((num_ba - 1,)),
+            dma((8,)),
+            dma((8,)),
+        ],
+        compiler_params=pltpu.CompilerParams(
+            collective_id=0, has_side_effects=True, vmem_limit_bytes=58 * 1024 * 1024
+        ),
+        cost_estimate=pl.CostEstimate(
+            flops=2 * num_freq * rows * columns * num_k * bands,
+            bytes_accessed=2 * num_freq * rows * columns,
+            transcendentals=0,
+        ),
+    )(pairs, dielectric, freq_weight, shells.reshape(1, width))
+
+
 def solution(mesh):
     in_specs = (P("ba", None, "ga"), P(None, "ga", None), P(None, "ba"), P("ga"))
     out_specs = P(None, "ba", None)
-    return jax.shard_map(local, mesh=mesh, in_specs=in_specs, out_specs=out_specs, check_vma=False)
+    num_ga, num_ba = mesh.shape["ga"], mesh.shape["ba"]
+
+    def run(pairs, dielectric, freq_weight, shells):
+        num_k, bands, width = pairs.shape
+        num_freq = dielectric.shape[0]
+        fits = num_ga == 8 and width % 128 == 0 and num_k % CHUNKS == 0
+        fits = fits and num_freq % 2 == 0 and bands == 64 and bands % (8 * num_ba) == 0
+        if fits:
+            return fused(pairs, dielectric, freq_weight, shells, num_ba)
+        return local(pairs, dielectric, freq_weight, shells)
+
+    return jax.shard_map(run, mesh=mesh, in_specs=in_specs, out_specs=out_specs, check_vma=False)

time: 161 us -> 54.4 us (0.34)
  waiting for transfers between devices: 82.9 us -> 0 us
  Pallas kernels: 0 us -> 52.9 us
  matrix products: 27.6 us -> 0 us
  blocking collectives: 22.3 us -> 0 us
  between operations: 14.1 us -> 0.01 us
  local copies, waits for them, and re-layouts: 11.2 us -> 1.38 us
  other arithmetic: 2.91 us -> 0 us
    pallas_call x0 -> x1, Pallas kernels: none -> 52.9 us  [fused(): pl.pallas_call(kernel, out_shape=jax.ShapeDtypeStruct((num_freq, piece, b...]
    all_gather x1 -> x0, waiting for transfers between devices: 49.5 us -> none  [local(): piece = lax.all_gather(scaled, 'ga', axis=2, tiled=True)]
    unnamed x3 -> x0, waiting for transfers between devices: 33.4 us -> none
    dot_general x2 -> x0, matrix products: 27.6 us -> none  [the longest x1 20.2 us: local(): lax.dot_general(row_matrix, flat_piece, (((1,), (1,)), ((), ())), preferr...]
    psum x1 -> x0, blocking collectives: 22.3 us -> none  [local(): summed = lax.psum(partial_value, 'ga')]
    reshape x1 -> x0, local copies, waits for them, and re-layouts: 8.48 us -> none  [local(): applied = applied.reshape(num_freq, local_rows, summed_bands, bands)]
    convert_element_type x1 -> x0, other arithmetic: 2.22 us -> none  [local(): scaled = (pairs.astype(jnp.float32) * coulomb).astype(jnp.bfloat16)]
  transfers between devices with their start and end apart: 2 -> 0, of which waited for: 2 -> 0; matrix products, arithmetic and copies ran while one was open for 0% -> 0% of each run, Pallas kernels for 0% -> 0%
where the time goes in v1:
time: 54.4 us; the launch traced here: 54.3 us
  Pallas kernels  52.9 us (97%)
  local copies, waits for them, and re-layouts  1.38 us (3%)
    pallas_call x1, Pallas kernels, fused(): pl.pallas_call(kernel, out_shape=jax.ShapeDtypeStruct((num_freq, piece, b...  52.9 us
    unnamed x1, local copies, waits for them, and re-layouts  1.38 us

profile of v1, /device:TPU:0, one launch (start us, length us, event | category | flops | bytes accessed | tf_op | source)
XLA Modules:
  0.0 54.3 jit_solution(4903708251088231061)
XLA Ops:
  0.0 52.9 %shard_map.46 = f32[4,16,64]{2,1,0:T(8,128)} custom-call(bf16[12,64,512]{2,1,0:T(8,128)(2,1)} %pairs_hbm.1, bf16[4,512,4096]{2,1,0:T(8,128)(2,1)} %d_hbm.1, f32[4,12]{1,0:T(4,128)} %w_ref.1, s32[1,512]{1,0:T(1,128)} %bitcast.1), custom_call_target="tpu_custom_call" | custom-call | flops 12884901888 | bytes 16777216 | tf_op jit(solution)/shard_map/pallas_call | solution.py:311
  52.9 1.4 %copy.6 = f32[4,16,64]{2,1,0:T(8,128)} copy(f32[4,16,64]{2,1,0:T(8,128)} %shard_map.46) | data formatting | bytes 32768

commit v2 on v1

--- a/solution.py
+++ b/solution.py
@@ -37,13 +37,14 @@
 
 def kernel(
     pairs_hbm, d_hbm, w_ref, shells_ref, out_ref,
-    raw, s, d, acc_a, hl, acc, acc_t, red_src, red_recv, red_all,
+    raw, s, d, acc_a, hl, acc, red_src, red_recv, red_all,
     pairs_sem, d_sem, send_sem, recv_sem, relay_send, red_send, red_rsem, all_send, all_rsem,
 ):
     num_k, bands, width = raw.shape
     num_freq = d.shape[1]
     num_ba = red_src.shape[0]
-    per = num_k // CHUNKS
+    part = width // CHUNKS
+    half = width // 2
     a = lax.axis_index("ga")
     b = lax.axis_index("ba")
     y, x, c = a // 4, (a // 2) % 2, a % 2
@@ -60,12 +61,14 @@
     pairs_copies = []
     for j in range(CHUNKS):
         copy = pltpu.make_async_copy(
-            pairs_hbm.at[pl.ds(j * per, per)], raw.at[pl.ds(j * per, per)], pairs_sem.at[j]
+            pairs_hbm.at[:, :, pl.ds(j * part, part)],
+            raw.at[:, :, pl.ds(j * part, part)],
+            pairs_sem.at[j],
         )
         copy.start()
         pairs_copies.append(copy)
     d_copies = {}
-    for slot in (0, 1, 6, 7, 2, 4, 3, 5):
+    for slot in (6, 0, 1, 7, 2, 4, 3, 5):
         columns = pl.ds(pl.multiple_of(partner(slot) * width, width), width)
         d_copies[slot] = pltpu.make_async_copy(d_hbm.at[:, :, columns], d.at[slot], d_sem.at[slot])
         d_copies[slot].start()
@@ -82,16 +85,17 @@
 
     def scale(j):
         pairs_copies[j].wait()
-        rows = pl.ds(j * per, per)
-        wide = raw[rows].reshape(per * bands, width).astype(jnp.float32) * coulomb
-        s[0, rows] = wide.astype(jnp.bfloat16).reshape(per, bands, width)
+        columns = pl.ds(j * part, part)
+        wide = raw[:, :, columns].reshape(num_k * bands, part).astype(jnp.float32)
+        wide = wide * coulomb[:, j * part : (j + 1) * part]
+        s[0, :, :, columns] = wide.astype(jnp.bfloat16).reshape(num_k, bands, part)
 
     def send(src_slot, mask, dst_slot, j, sem):
-        rows = pl.ds(j * per, per)
+        columns = pl.ds(j * part, part)
         target = relay_to if mask is None else partner(mask)
         copy = pltpu.make_async_remote_copy(
-            src_ref=s.at[src_slot, rows],
-            dst_ref=s.at[dst_slot, rows],
+            src_ref=s.at[src_slot, :, :, columns],
+            dst_ref=s.at[dst_slot, :, :, columns],
             send_sem=sem,
             recv_sem=recv_sem.at[dst_slot, j],
             device_id={"ga": target},
@@ -111,9 +115,9 @@
         if slot == 0 or (slot, j) in arrived:
             return
         arrived.add((slot, j))
-        rows = pl.ds(j * per, per)
+        columns = pl.ds(j * part, part)
         pltpu.make_async_remote_copy(
-            src_ref=s.at[slot, rows], dst_ref=s.at[slot, rows],
+            src_ref=s.at[slot, :, :, columns], dst_ref=s.at[slot, :, :, columns],
             send_sem=send_sem.at[slot, j], recv_sem=recv_sem.at[slot, j],
             device_id={"ga": partner(1)}, device_id_type=MESH,
         ).wait_recv()
@@ -136,64 +140,69 @@
         wait(6, j)
         forward(6, 1, 7, j)
 
-    def apply_h(slots, first, parts):
+    def apply_h(slots, start, size, freqs, first=False):
         for slot in slots:
             need(slot)
-        size = per * parts[1]
-        start = parts[0] * per
+        columns = pl.ds(start, size)
 
         def body(f, carry):
             total = None
             for slot in slots:
-                left = s[slot, pl.ds(start, size)].reshape(size * bands, width)
-                term = lax.dot_general(left, d[slot, f], NT, preferred_element_type=jnp.float32)
+                left = s[slot, :, :, columns].reshape(num_k * bands, size)
+                term = lax.dot_general(
+                    left, d[slot, f, :, columns], NT, preferred_element_type=jnp.float32
+                )
                 total = term if total is None else total + term
-            total = total.reshape(size, bands, width)
+            total = total.reshape(num_k, bands, width)
             if first:
-                acc_a[pl.ds(start, size), f] = total
+                acc_a[:, f] = total
             else:
-                acc_a[pl.ds(start, size), f] += total
+                acc_a[:, f] += total
             return carry
 
-        lax.fori_loop(0, num_freq, body, 0)
-
-    def split(which, rows, f, wide):
+        lax.fori_loop(*freqs, body, 0)
+
+    def split(wide):
         high = wide.astype(jnp.bfloat16)
-        low = (wide - high.astype(jnp.float32)).astype(jnp.bfloat16)
-        hl[which, rows, 0, f] = high
-        hl[which, rows, 1, f] = low
-
-    def apply_g(which, slot, half):
+        return high, (wide - high.astype(jnp.float32)).astype(jnp.bfloat16)
+
+    def apply_g(which, slot, freqs):
         need(slot)
-        size = num_k // 2
-        rows = pl.ds(half * size, size)
 
         def body(f, carry):
             wide = lax.dot_general(
-                s[0, rows].reshape(size * bands, width), d[slot, f], NN,
+                s[0].reshape(num_k * bands, width), d[slot, f], NN,
                 preferred_element_type=jnp.float32,
             )
-            split(which, rows, f, wide.reshape(size, bands, width))
+            high, low = split(wide.reshape(num_k, bands, width))
+            hl[which, :, 0, f] = high
+            hl[which, :, 1, f] = low
             return carry
 
-        lax.fori_loop(0, num_freq, body, 0)
-
-    def second(which, slot, target, j):
-        def body(k, carry):
-            left = hl[which, k].reshape(2 * num_freq * bands, width)
-            both = lax.dot_general(left, s[slot, k], NT, preferred_element_type=jnp.float32)
-            both = both.reshape(2, num_freq, bands, bands)
-            both = both[0] + both[1]
-            return tuple(carry[f] + w_ref[f, k] * both[f] for f in range(num_freq))
-
-        terms = tuple(target[f] for f in range(num_freq))
-        for k in range(j * per, (j + 1) * per):
-            terms = body(k, terms)
+        lax.fori_loop(*freqs, body, 0)
+
+    def add_second(terms, k, left, right):
+        both = lax.dot_general(left, right, NT, preferred_element_type=jnp.float32)
+        both = both.reshape(2, num_freq, bands, bands)
+        both = both[0] + both[1]
+        return tuple(terms[f] + w_ref[f, k] * both[f] for f in range(num_freq))
+
+    def second(which, slot, start, size):
+        terms = tuple(acc[f] for f in range(num_freq))
+        columns = pl.ds(start, size)
+        for k in range(num_k):
+            left = hl[which, k, :, :, :, columns].reshape(2 * num_freq * bands, size)
+            terms = add_second(terms, k, left, s[slot, k, :, columns])
         for f in range(num_freq):
-            target[f] = terms[f]
-
-    acc[...] = jnp.zeros_like(acc)
-    acc_t[...] = jnp.zeros_like(acc_t)
+            acc[f] = terms[f]
+
+    def second_own():
+        terms = tuple(jnp.zeros((bands, bands), jnp.float32) for f in range(num_freq))
+        for k in range(num_k):
+            high, low = split(acc_a[k].reshape(num_freq * bands, width))
+            terms = add_second(terms, k, jnp.concatenate([high, low], axis=0), s[0, k])
+        for f in range(num_freq):
+            acc[f] = terms[f].T
 
     scale(0)
     pl.semaphore_wait(barrier, 7 + num_ba - 1)
@@ -204,60 +213,48 @@
         forward(0, 4, 4, j)
         started.append(send(0, 1, 1, j, relay_send.at[j]))
 
+    low_f, high_f = (0, num_freq // 2), (num_freq // 2, num_freq)
+    every_f = (0, num_freq)
+    apply_g(0, 6, every_f)
     for j in range(CHUNKS):
         wait(1, j)
-    apply_h((0, 1), True, (0, CHUNKS))
+    apply_h((0, 1), 0, width, low_f, True)
     arrive(0)
-    apply_h((2, 4), False, (0, 1))
-    apply_g(0, 6, 0)
-    apply_g(0, 6, 1)
+    apply_h((0, 1), 0, width, high_f, True)
+    apply_g(1, 7, low_f)
     arrive(1)
-    wait(3, 0)
-    wait(5, 0)
-    apply_h((2, 4), False, (1, 1))
-    apply_h((3, 5), False, (0, 1))
-    apply_g(1, 7, 0)
+    apply_g(1, 7, high_f)
+    apply_h((2, 4), 0, half, every_f)
+    for j in (0, 1):
+        wait(3, j)
+        wait(5, j)
+    apply_h((3, 5), 0, half, low_f)
     arrive(2)
-    apply_g(1, 7, 1)
-    wait(3, 1)
-    wait(5, 1)
-    apply_h((3, 5), False, (1, 1))
+    apply_h((3, 5), 0, half, high_f)
     arrive_far(0)
-    apply_h((2, 4), False, (2, 1))
     arrive(3)
-    wait(3, 2)
-    wait(5, 2)
-    apply_h((3, 5), False, (2, 1))
+    apply_h((2, 4), half, half, every_f)
     arrive_far(1)
-    apply_h((2, 4), False, (3, 1))
-    wait(3, 3)
-    wait(5, 3)
-    apply_h((3, 5), False, (3, 1))
-    for j in range(CHUNKS):
-        rows = pl.ds(j * per, per)
-        for f in range(num_freq):
-            split(2, rows, f, acc_a[rows, f])
-        second(2, 0, acc_t, j)
-        if j == 1:
-            second(0, 6, acc, 0)
-            second(0, 6, acc, 1)
-            arrive_far(2)
-    wait(7, 0)
-    second(1, 7, acc, 0)
-    wait(7, 1)
-    second(1, 7, acc, 1)
-    second(0, 6, acc, 2)
+    for j in (2, 3):
+        wait(3, j)
+        wait(5, j)
+    apply_h((3, 5), half, half, every_f)
+    second_own()
+    arrive_far(2)
+    second(0, 6, 0, half)
+    for j in (0, 1):
+        wait(7, j)
+    second(1, 7, 0, half)
     arrive_far(3)
-    wait(7, 2)
-    second(1, 7, acc, 2)
-    second(0, 6, acc, 3)
-    wait(7, 3)
-    second(1, 7, acc, 3)
+    second(0, 6, half, half)
+    for j in (2, 3):
+        wait(7, j)
+    second(1, 7, half, half)
 
     piece = bands // num_ba
     for pair in range(num_freq // 2):
-        first_f = acc[2 * pair] + acc_t[2 * pair].T
-        second_f = acc[2 * pair + 1] + acc_t[2 * pair + 1].T
+        first_f = acc[2 * pair]
+        second_f = acc[2 * pair + 1]
         both = jnp.concatenate([first_f, second_f], axis=1)
         red_src[:, pair] = both.reshape(num_ba, piece, 2 * bands)
 
@@ -323,8 +320,7 @@
             pltpu.VMEM((8, num_k, bands, width), bf16),
             pltpu.VMEM((8, num_freq, rows, width), bf16),
             pltpu.VMEM((num_k, num_freq, bands, width), f32),
-            pltpu.VMEM((3, num_k, 2, num_freq, bands, width), bf16),
-            pltpu.VMEM((num_freq, bands, bands), f32),
+            pltpu.VMEM((2, num_k, 2, num_freq, bands, width), bf16),
             pltpu.VMEM((num_freq, bands, bands), f32),
             pltpu.VMEM((num_ba, num_freq // 2, piece, 2 * bands), f32),
             pltpu.VMEM((num_ba - 1, num_freq // 2, piece, 2 * bands), f32),
@@ -358,7 +354,7 @@
     def run(pairs, dielectric, freq_weight, shells):
         num_k, bands, width = pairs.shape
         num_freq = dielectric.shape[0]
-        fits = num_ga == 8 and width % 128 == 0 and num_k % CHUNKS == 0
+        fits = num_ga == 8 and width % (128 * CHUNKS) == 0
         fits = fits and num_freq % 2 == 0 and bands == 64 and bands % (8 * num_ba) == 0
         if fits:
             return fused(pairs, dielectric, freq_weight, shells, num_ba)

time: 54.4 us -> 48.1 us (0.88)
  Pallas kernels: 52.9 us -> 46.6 us
    pallas_call x1, Pallas kernels: 52.9 us -> 46.6 us  [fused(): pl.pallas_call(kernel, out_shape=jax.ShapeDtypeStruct((num_freq, piece, b...]
where the time goes in v2:
time: 48.1 us; the launch traced here: 47.9 us
  Pallas kernels  46.6 us (97%)
  local copies, waits for them, and re-layouts  1.38 us (3%)
    pallas_call x1, Pallas kernels, fused(): pl.pallas_call(kernel, out_shape=jax.ShapeDtypeStruct((num_freq, piece, b...  46.6 us
    unnamed x1, local copies, waits for them, and re-layouts  1.38 us

profile of v2, /device:TPU:0, one launch (start us, length us, event | category | flops | bytes accessed | tf_op | source)
XLA Modules:
  0.0 47.9 jit_solution(13365811631731075091)
XLA Ops:
  0.0 46.6 %shard_map.46 = f32[4,16,64]{2,1,0:T(8,128)} custom-call(bf16[12,64,512]{2,1,0:T(8,128)(2,1)} %pairs_hbm.1, bf16[4,512,4096]{2,1,0:T(8,128)(2,1)} %d_hbm.1, f32[4,12]{1,0:T(4,128)} %w_ref.1, s32[1,512]{1,0:T(1,128)} %bitcast.1), custom_call_target="tpu_custom_call" | custom-call | flops 12884901888 | bytes 16777216 | tf_op jit(solution)/shard_map/pallas_call | solution.py:308
  46.6 1.4 %copy.6 = f32[4,16,64]{2,1,0:T(8,128)} copy(f32[4,16,64]{2,1,0:T(8,128)} %shard_map.46) | data formatting | bytes 32768

commit v3 on v2

--- a/solution.py
+++ b/solution.py
@@ -239,17 +239,13 @@
         wait(3, j)
         wait(5, j)
     apply_h((3, 5), half, half, every_f)
+    arrive_far(2)
     second_own()
-    arrive_far(2)
-    second(0, 6, 0, half)
-    for j in (0, 1):
+    arrive_far(3)
+    second(0, 6, 0, width)
+    for j in range(CHUNKS):
         wait(7, j)
-    second(1, 7, 0, half)
-    arrive_far(3)
-    second(0, 6, half, half)
-    for j in (2, 3):
-        wait(7, j)
-    second(1, 7, half, half)
+    second(1, 7, 0, width)
 
     piece = bands // num_ba
     for pair in range(num_freq // 2):

time: 48.1 us -> 47.6 us (0.990)
  Pallas kernels: 46.6 us -> 46.1 us
    pallas_call x1, Pallas kernels: 46.6 us -> 46.1 us  [fused(): pl.pallas_call(kernel, out_shape=jax.ShapeDtypeStruct((num_freq, piece, b...]
where the time goes in v3:
time: 47.6 us; the launch traced here: 47.4 us
  Pallas kernels  46.1 us (97%)
  local copies, waits for them, and re-layouts  1.38 us (3%)
    pallas_call x1, Pallas kernels, fused(): pl.pallas_call(kernel, out_shape=jax.ShapeDtypeStruct((num_freq, piece, b...  46.1 us
    unnamed x1, local copies, waits for them, and re-layouts  1.38 us

profile of v3, /device:TPU:0, one launch (start us, length us, event | category | flops | bytes accessed | tf_op | source)
XLA Modules:
  0.0 47.4 jit_solution(18355449447554451315)
XLA Ops:
  0.0 46.1 %shard_map.46 = f32[4,16,64]{2,1,0:T(8,128)} custom-call(bf16[12,64,512]{2,1,0:T(8,128)(2,1)} %pairs_hbm.1, bf16[4,512,4096]{2,1,0:T(8,128)(2,1)} %d_hbm.1, f32[4,12]{1,0:T(4,128)} %w_ref.1, s32[1,512]{1,0:T(1,128)} %bitcast.1), custom_call_target="tpu_custom_call" | custom-call | flops 12884901888 | bytes 16777216 | tf_op jit(solution)/shard_map/pallas_call | solution.py:304
  46.1 1.4 %copy.6 = f32[4,16,64]{2,1,0:T(8,128)} copy(f32[4,16,64]{2,1,0:T(8,128)} %shard_map.46) | data formatting | bytes 32768
